TPU v7x, 128 devices: a whole 4x4x4 slice. The times are simulated.
128 devices in a mesh: slab: 4 (over y), cube: 32 (over x, z, core).
Axes of the slice: x: 4, y: 4, z: 4, core: 2. Of those that a mesh axis runs over, the one named last changes fastest.
Arguments:
- owned_part: bfloat16 [4096, 64, 384], P(('slab', 'cube')), may hold values from -6 to 6
- shared_part: bfloat16 [4096, 64, 384], P(('slab', 'cube')), may hold values from -6 to 6
- shared_cube: int32 [4096, 1], P(('slab', 'cube')), may hold values from 0 to 31; in each aligned block of 32 rows (0 to 31, 32 to 63, ...) at most 2 rows name the same one
- shared_octant: int32 [4096], P(('slab', 'cube')), may hold values from 0 to 31
- interaction: int32 [4096, 4, 8], P(('slab', 'cube')), may hold values from 0 to 31
- operators: bfloat16 [32, 384, 384], replicated, may hold values from -0.0546875 to 0.0546875
Outputs:
- far_field: bfloat16 [4096, 64, 384], P(('slab', 'cube'))
Inputs may be any that keep to these rules, and one draw needn't show every extreme that they name: `shared_cube`: among the 32 rows of one device no cube index is named by more than 2 rows, and some cube index is named by exactly 2 rows.
All inputs are finite; a program needn't handle non-finite values.
Results may differ from a plain program's by a relative error of at most 0.0048.
Values may be sent and summed in bfloat16 or wider, within the bound.
A program may use at most 256 MiB of HBM per device.

v0:
```python
import jax
import jax.numpy as jnp
from jax import lax
from jax.sharding import PartitionSpec as P

LPS = 8
CAP = 2


def swapped(value, axis, distance):
    mask = 2**distance
    pairs = [(source, source ^ mask) for source in range(lax.axis_size(axis))]
    return lax.ppermute(value, axis, pairs)


def body(owned_part, shared_part, shared_cube, shared_octant, interaction, operators):
    octant_count = owned_part.shape[0]
    rhs_count = owned_part.shape[1]
    coeff_count = owned_part.shape[2]
    slot_count = shared_part.shape[0]
    row_width = rhs_count * coeff_count
    cube_count = lax.axis_size("cube")
    owner_cube = shared_cube[:, 0]
    slot_order = jnp.arange(slot_count, dtype=jnp.int32)
    earlier = (owner_cube[:, None] == owner_cube[None, :]) & (
        slot_order[None, :] < slot_order[:, None]
    )
    slot_rank = jnp.sum(earlier.astype(jnp.int32), axis=1)
    position = owner_cube * CAP + slot_rank
    placing = jnp.arange(cube_count * CAP, dtype=jnp.int32)[:, None] == position[None, :]
    packed = jnp.dot(
        placing.astype(jnp.bfloat16),
        shared_part.reshape(slot_count, row_width),
        preferred_element_type=jnp.float32,
    ).astype(jnp.bfloat16)
    labels = jnp.sum(jnp.where(placing, shared_octant[None, :] + 1, 0), axis=1) - 1
    buffer = packed.reshape(cube_count, 1, CAP, row_width)
    markers = labels.reshape(cube_count, 1, CAP)
    my_index = lax.axis_index("cube")
    section_count = cube_count.bit_length() - 1
    for section_bit in range(section_count - 1, -1, -1):
        half_count = buffer.shape[0] // 2
        buffer = buffer.reshape((2, half_count) + buffer.shape[1:])
        markers = markers.reshape((2, half_count) + markers.shape[1:])
        my_bit = my_index >> section_bit & 1
        retained = lax.dynamic_index_in_dim(buffer, my_bit, 0, keepdims=False)
        outgoing = lax.dynamic_index_in_dim(buffer, 1 - my_bit, 0, keepdims=False)
        kept_markers = lax.dynamic_index_in_dim(markers, my_bit, 0, keepdims=False)
        sent_markers = lax.dynamic_index_in_dim(markers, 1 - my_bit, 0, keepdims=False)
        incoming, incoming_markers = swapped((outgoing, sent_markers), "cube", section_bit)
        buffer = jnp.concatenate([retained, incoming], axis=1)
        markers = jnp.concatenate([kept_markers, incoming_markers], axis=1)
    arrived = buffer.reshape(cube_count * CAP, row_width)
    labels_in = markers.reshape(cube_count * CAP)
    member = (jnp.arange(octant_count, dtype=jnp.int32)[:, None] == labels_in[None, :]).astype(
        jnp.bfloat16
    )
    summed = jnp.dot(member, arrived, preferred_element_type=jnp.float32) + owned_part.reshape(
        octant_count, row_width
    ).astype(jnp.float32)
    density = summed.astype(jnp.bfloat16).reshape(octant_count, rhs_count, coeff_count)
    initial = jnp.zeros((octant_count, rhs_count, coeff_count), jnp.float32)
    running = initial
    shard_block = lax.all_gather(density, "slab", axis=0, tiled=True)
    first_row = jnp.int32(0)
    shard_total = shard_block.shape[0] // octant_count
    for shard_pos in range(shard_total):
        slab_now = first_row // octant_count + shard_pos
        shard_rows = shard_block[shard_pos * octant_count : (shard_pos + 1) * octant_count]
        sources = lax.dynamic_index_in_dim(interaction, slab_now, 1, keepdims=False)
        for entry in range(LPS):
            selected = jnp.take(shard_rows, sources[:, entry], axis=0).reshape(
                octant_count * rhs_count, coeff_count
            )
            operator_now = lax.dynamic_index_in_dim(
                operators, slab_now * LPS + entry, 0, keepdims=False
            )
            running = running + jnp.dot(
                selected, operator_now, preferred_element_type=jnp.float32
            ).reshape(running.shape)
    return running.astype(jnp.bfloat16)


def solution(mesh):
    placed = (
        P(("slab", "cube"), None, None),
        P(("slab", "cube"), None, None),
        P(("slab", "cube"), None),
        P(("slab", "cube")),
        P(("slab", "cube"), None, None),
        P(),
    )
    return jax.shard_map(
        body, mesh=mesh, in_specs=placed, out_specs=P(("slab", "cube"), None, None), check_vma=False
    )
```

profile of v0, /device:TPU:0, one launch (start us, length us, event | category | flops | bytes accessed | tf_op | source)
XLA Modules:
  0.0 518.6 jit_solution(16381503860820578917)
XLA Ops:
  11.0 3.4 reshape_reshape.4
  14.3 6.1 %constant_dynamic-slice_fusion.6 = (bf16[1,16,1,2,24576]{4,3,1,0,2:T(2,128)(2,1)S(1)}, bf16[16,1,2,24576]{3,2,0,1:T(2,128)(2,1)}) fusion(bf16[2,16,1,2,24576]{4,3,1,0,2:T(2,128)(2,1)} %reshape_reshape.4, s32[]{:T(128)S(6)} %select_n.106, s32[]{:T(128)S(6)} %select_n.107), kind=kLoop, calls=%fused_computation.269 | loop fusion | bytes 6291464 | tf_op jit(solution)/shard_map/jit(dynamic_index_in_dim)/dynamic_slice | solution.py:46
  23.5 34.6 %collective-permute-done.5 = bf16[16,1,2,24576]{3,2,0,1:T(2,128)(2,1)S(1)} collective-permute-done((bf16[16,1,2,24576]{3,2,0,1:T(2,128)(2,1)}, bf16[16,1,2,24576]{3,2,0,1:T(2,128)(2,1)S(1)}, u32[]{:S(2)}, u32[]{:S(2)}) %collective-permute-start.5) | collective-permute-done | bytes 1572896 | tf_op jit(solution)/shard_map/ppermute | solution.py:13
  59.2 6.5 %fusion.8 = (bf16[1,8,2,2,24576]{4,3,1,0,2:T(2,128)(2,1)S(1)}, bf16[8,2,2,24576]{3,2,0,1:T(2,128)(2,1)}) fusion(s32[]{:T(128)S(6)} %select_n.108, bf16[2,8,1,2,24576]{4,3,1,0,2:T(2,128)(2,1)S(1)} %bitcast.286, bf16[2,8,1,2,24576]{4,3,1,0,2:T(2,128)(2,1)} %bitcast.289, s32[]{:T(128)S(6)} %select_n.109), kind=kLoop, calls=%fused_computation.60 | loop fusion | flops 1572864 | bytes 6291464 | tf_op jit(solution)/shard_map/concatenate | solution.py:51
  67.4 33.7 %collective-permute-done.6 = bf16[8,2,2,24576]{3,2,0,1:T(2,128)(2,1)S(1)} collective-permute-done((bf16[8,2,2,24576]{3,2,0,1:T(2,128)(2,1)}, bf16[8,2,2,24576]{3,2,0,1:T(2,128)(2,1)S(1)}, u32[]{:S(2)}, u32[]{:S(2)}) %collective-permute-start.6) | collective-permute-done | bytes 1572896 | tf_op jit(solution)/shard_map/ppermute | solution.py:13
  102.3 5.9 %fusion.6 = (bf16[1,4,4,2,24576]{4,3,1,0,2:T(2,128)(2,1)S(1)}, bf16[4,4,2,24576]{3,2,0,1:T(2,128)(2,1)}) fusion(s32[]{:T(128)S(6)} %select_n.110, bf16[2,4,2,2,24576]{4,3,1,0,2:T(2,128)(2,1)S(1)} %bitcast.284, bf16[2,4,2,2,24576]{4,3,1,0,2:T(2,128)(2,1)} %bitcast.290, s32[]{:T(128)S(6)} %select_n.111), kind=kLoop, calls=%fused_computation.58 | loop fusion | flops 1572864 | bytes 6291464 | tf_op jit(solution)/shard_map/concatenate | solution.py:51
  108.3 4.1 collective-permute-start.7
  112.4 32.8 %collective-permute-done.7 = bf16[4,4,2,24576]{3,2,0,1:T(2,128)(2,1)S(1)} collective-permute-done((bf16[4,4,2,24576]{3,2,0,1:T(2,128)(2,1)}, bf16[4,4,2,24576]{3,2,0,1:T(2,128)(2,1)S(1)}, u32[]{:S(2)}, u32[]{:S(2)}) %collective-permute-start.7) | collective-permute-done | bytes 1572896 | tf_op jit(solution)/shard_map/ppermute | solution.py:13
  146.3 5.9 %fusion.75 = (bf16[2,8,2,24576]{3,2,0,1:T(2,128)(2,1)}, bf16[2,8,2,24576]{3,2,0,1:T(2,128)(2,1)S(1)}) fusion(s32[]{:T(128)S(6)} %select_n.113, bf16[2,2,4,2,24576]{4,3,1,0,2:T(2,128)(2,1)} %bitcast.291, bf16[2,2,4,2,24576]{4,3,1,0,2:T(2,128)(2,1)S(1)} %bitcast.285, s32[]{:T(128)S(6)} %select_n.112), kind=kLoop, calls=%fused_computation.128 | loop fusion | flops 1572864 | bytes 6291464 | tf_op jit(solution)/shard_map/jit(dynamic_index_in_dim)/squeeze | solution.py:47
  153.8 32.6 %collective-permute-done.8 = bf16[2,8,2,24576]{3,2,0,1:T(2,128)(2,1)S(1)} collective-permute-done((bf16[2,8,2,24576]{3,2,0,1:T(2,128)(2,1)}, bf16[2,8,2,24576]{3,2,0,1:T(2,128)(2,1)S(1)}, u32[]{:S(2)}, u32[]{:S(2)}) %collective-permute-start.8) | collective-permute-done | bytes 1572896 | tf_op jit(solution)/shard_map/ppermute | solution.py:13
  187.5 6.3 %fusion.2 = (bf16[1,16,2,24576]{3,2,0,1:T(2,128)(2,1)}, bf16[1,16,2,24576]{3,2,0,1:T(2,128)(2,1)}) fusion(s32[]{:T(128)S(6)} %select_n.114, bf16[2,8,2,24576]{3,2,0,1:T(2,128)(2,1)S(1)} %get-tuple-element.77, bf16[2,8,2,24576]{3,2,0,1:T(2,128)(2,1)} %copy-done.31, s32[]{:T(128)S(6)} %select_n.115), kind=kLoop, calls=%fused_computation.54 | loop fusion | flops 1572864 | bytes 6291464 | tf_op jit(solution)/shard_map/concatenate | solution.py:51
  216.1 5.9 %pad_maximum_fusion = bf16[1,32,2,24576]{3,2,0,1:T(2,128)(2,1)S(1)} fusion(bf16[1,16,2,24576]{3,2,0,1:T(2,128)(2,1)} %copy-done.30, bf16[1,16,2,24576]{3,2,0,1:T(2,128)(2,1)} %get-tuple-element.74), kind=kLoop, calls=%fused_computation.35 | loop fusion | flops 1572864 | bytes 6291456 | tf_op jit(solution)/shard_map/concatenate | solution.py:51
  225.1 3.4 fusion
  231.2 66.3 %all-gather.2.cloned.1.call-done = bf16[128,64,384]{2,1,0:T(8,128)(2,1)} async-done(((bf16[32,64,384]{2,1,0:T(8,128)(2,1)}), bf16[128,64,384]{2,1,0:T(8,128)(2,1)}) %all-gather.2.cloned.1.call-update) | async-done | bytes 6291472 | tf_op jit(solution)/shard_map/all_gather | solution.py:64
  297.5 5.5 %fusion.249 = (bf16[32,64,384]{2,1,0:T(8,128)(2,1)}, bf16[32,64,384]{2,1,0:T(8,128)(2,1)}, bf16[32,64,384]{2,1,0:T(8,128)(2,1)S(1)}, bf16[32,64,384]{2,1,0:T(8,128)(2,1)S(1)}) fusion(bf16[128,64,384]{2,1,0:T(8,128)(2,1)} %all-gather.2.cloned.1.call-done), kind=kLoop, calls=%fused_computation.430 | loop fusion | bytes 12582912 | tf_op jit(solution)/shard_map/slice | solution.py:69
  303.0 3.4 gather_fusion.7
  306.3 3.3 gather_fusion.6
  316.3 3.4 gather_fusion.3
  319.7 3.3 gather_fusion.2
  323.0 3.3 gather_fusion.1
  329.7 3.4 gather_fusion.31
  336.3 3.4 gather_fusion.29
  339.7 3.3 gather_fusion.28
  343.0 3.4 gather_fusion.27
  346.4 3.3 gather_fusion.26
  349.7 3.3 gather_fusion.25
  353.1 3.3 gather_fusion.24
  389.0 4.6 fusion.52
  393.6 3.9 fusion.50
  397.5 4.0 fusion.48
  401.5 4.0 fusion.46
  480.5 30.8 %add_convert_fusion = bf16[32,64,384]{2,1,0:T(8,128)(2,1)} fusion(f32[32,64,384]{2,1,0:T(8,128)} %fusion.10, f32[32,64,384]{2,1,0:T(8,128)} %fusion.12, f32[32,64,384]{2,1,0:T(8,128)} %fusion.14, f32[32,64,384]{2,1,0:T(8,128)} %fusion.16, f32[32,64,384]{2,1,0:T(8,128)} %fusion.18, f32[32,64,384]{2,1,0:T(8,128)} %fusion.20, f32[32,64,384]{2,1,0:T(8,128)} %fusion.22, ...), kind=kOutput, calls=%fused_computation.36 | convolution fusion | flops 629932032 | bytes 100958240 | tf_op jit(solution)/shard_map/dot_general | solution.py:78
  (210 shorter events, 163.6 us)
Async XLA Ops:
  6.5 290.9 %all-gather.2.cloned.1.call-start = ((), (), s32[]{:S(2)}) async-start(), calls=%async_computation | async-start | bytes 7864320 | tf_op jit(solution)/shard_map/all_gather | solution.py:64
  20.4 37.7 %collective-permute-start.5 = (bf16[16,1,2,24576]{3,2,0,1:T(2,128)(2,1)}, bf16[16,1,2,24576]{3,2,0,1:T(2,128)(2,1)S(1)}, u32[]{:S(2)}, u32[]{:S(2)}) collective-permute-start(bf16[16,1,2,24576]{3,2,0,1:T(2,128)(2,1)} %get-tuple-element.83), channel_id=1, source_target_pairs={{0,16},{1,17},{2,18},{3,19},{4,20},{5,21},{6,22},{7,23},{8,24},{9,... | collective-permute-start | bytes 4718600 | tf_op jit(solution)/shard_map/ppermute | solution.py:13
  65.7 35.4 %collective-permute-start.6 = (bf16[8,2,2,24576]{3,2,0,1:T(2,128)(2,1)}, bf16[8,2,2,24576]{3,2,0,1:T(2,128)(2,1)S(1)}, u32[]{:S(2)}, u32[]{:S(2)}) collective-permute-start(bf16[8,2,2,24576]{3,2,0,1:T(2,128)(2,1)} %get-tuple-element.81), channel_id=1, source_target_pairs={{0,8},{1,9},{2,10},{3,11},{4,12},{5,13},{6,14},{7,15},{8,0},{9,1},... | collective-permute-start | bytes 4718600 | tf_op jit(solution)/shard_map/ppermute | solution.py:13
  108.3 36.9 %collective-permute-start.7 = (bf16[4,4,2,24576]{3,2,0,1:T(2,128)(2,1)}, bf16[4,4,2,24576]{3,2,0,1:T(2,128)(2,1)S(1)}, u32[]{:S(2)}, u32[]{:S(2)}) collective-permute-start(bf16[4,4,2,24576]{3,2,0,1:T(2,128)(2,1)} %get-tuple-element.79), channel_id=1, source_target_pairs={{0,4},{1,5},{2,6},{3,7},{4,0},{5,1},{6,2},{7,3},{8,12},{9,13},{10,... | collective-permute-start | bytes 4718600 | tf_op jit(solution)/shard_map/ppermute | solution.py:13
  152.3 34.1 %collective-permute-start.8 = (bf16[2,8,2,24576]{3,2,0,1:T(2,128)(2,1)}, bf16[2,8,2,24576]{3,2,0,1:T(2,128)(2,1)S(1)}, u32[]{:S(2)}, u32[]{:S(2)}) collective-permute-start(bf16[2,8,2,24576]{3,2,0,1:T(2,128)(2,1)} %get-tuple-element.76), channel_id=1, source_target_pairs={{0,2},{1,3},{2,0},{3,1},{4,6},{5,7},{6,4},{7,5},{8,10},{9,11},{10,... | collective-permute-start | bytes 4718600 | tf_op jit(solution)/shard_map/ppermute | solution.py:13
  187.5 24.6 %copy-start.29 = (bf16[32,64,384]{2,1,0:T(8,128)(2,1)S(1)}, bf16[32,64,384]{2,1,0:T(8,128)(2,1)}, u32[]{:S(2)}) copy-start(bf16[32,64,384]{2,1,0:T(8,128)(2,1)} %param.8) | copy-start | bytes 4718596
  193.8 21.1 %collective-permute-start.9 = (bf16[1,16,2,24576]{3,2,0,1:T(2,128)(2,1)}, bf16[1,16,2,24576]{3,2,0,1:T(2,128)(2,1)S(1)}, u32[]{:S(2)}, u32[]{:S(2)}) collective-permute-start(bf16[1,16,2,24576]{3,2,0,1:T(2,128)(2,1)} %get-tuple-element.75), channel_id=1, source_target_pairs={{0,1},{1,0},{2,3},{3,2},{4,5},{5,4},{6,7},{7,6},{8,9},{9,8},{10,11... | collective-permute-start | bytes 4718600 | tf_op jit(solution)/shard_map/ppermute | solution.py:13
  194.1 5.1 collective-permute-start
  199.4 3.6 collective-permute-start.1
  203.2 5.1 collective-permute-start.2
  208.4 3.6 collective-permute-start.3
  212.1 2.6 collective-permute-start.4
  386.2 7.3 %copy-start.27 = (bf16[32,64,384]{2,1,0:T(8,128)(2,1)S(1)}, bf16[32,64,384]{2,1,0:T(8,128)(2,1)}, u32[]{:S(2)}) copy-start(bf16[32,64,384]{2,1,0:T(8,128)(2,1)} %gather_fusion.10) | copy-start | bytes 4718596
  386.2 19.3 %slice-start = ((s8[9437184]{0:T(1024)(128)(4,1)}), s8[4194304]{0:T(1024)(128)(4,1)S(1)}, s32[]{:S(2)}) async-start(s8[9437184]{0:T(1024)(128)(4,1)} %bitcast.279), calls=%async_computation.1 | async-start | bytes 8388608
  389.0 16.6 %slice-start.1 = ((s8[9437184]{0:T(1024)(128)(4,1)}), s8[4194304]{0:T(1024)(128)(4,1)S(1)}, s32[]{:S(2)}) async-start(s8[9437184]{0:T(1024)(128)(4,1)} %bitcast.279), calls=%async_computation.2 | async-start | bytes 8388608
  393.6 3.9 copy-start.26
  397.5 4.0 copy-start.25
  397.5 8.0 %slice-start.2 = ((s8[9437184]{0:T(1024)(128)(4,1)}), s8[1048576]{0:T(1024)(128)(4,1)S(1)}, s32[]{:S(2)}) async-start(s8[9437184]{0:T(1024)(128)(4,1)} %bitcast.279), calls=%async_computation.3 | async-start | bytes 2097152
  401.5 4.0 copy-start.24
  414.1 2.9 copy-start.21
  425.5 3.1 copy-start.17
  434.3 2.9 copy-start.14
  440.1 2.9 copy-start.12
  445.8 2.9 copy-start.10
  448.7 2.9 copy-start.9
  451.6 2.9 copy-start.8
  454.4 3.1 copy-start.7
  457.5 2.9 copy-start.6
  460.4 2.9 copy-start.5
  466.1 2.9 copy-start.3
  471.9 2.9 copy-start.1
  477.6 2.9 copy-start.28
  (20 other events, 45.2 us)
Sparse Core Ops, SparseCore 0:
  230.1 67.3 all-gather.1
where the time goes:
time: 528 us; the launch traced here: 519 us
  waiting for transfers between devices  209 us (40%)
  matrix products  129 us (24%)
  local copies, waits for them, and re-layouts  115 us (22%)
  other arithmetic  32.1 us (6%)
  starting transfers between devices  19 us (4%)
  between operations  14.4 us (3%)
    ppermute x10, waiting for transfers between devices, swapped(): return lax.ppermute(value, axis, pairs)  142 us
    dot_general x32, matrix products, body(): jnp.dot(selected, operator_now, preferred_element_type=jnp.float32)  125 us
    gather x32, local copies, waits for them, and re-layouts, body(): jnp.take(shard_rows, sources[:, entry], axis=0)  83.2 us
    all_gather x1, waiting for transfers between devices, body(): shard_block = lax.all_gather(density, 'slab', axis=0, tiled=True)  66.3 us
    concatenate x4, other arithmetic, body(): buffer = jnp.concatenate([retained, incoming], axis=1)  24.6 us
    ppermute x10, starting transfers between devices, swapped(): return lax.ppermute(value, axis, pairs)  19 us
    unnamed x86, local copies, waits for them, and re-layouts  12.9 us
  transfers between devices with their start and end apart: 11, of which 9 were waited for; matrix products, arithmetic and copies ran while one was open for 1% of the time, Pallas kernels for 0%

commit v1 on v0

v1 whole, which is shorter than its diff:
```python
import functools

import jax
import jax.numpy as jnp
from jax import lax
from jax.experimental import pallas as pl
from jax.experimental.pallas import tpu as pltpu
from jax.sharding import PartitionSpec as P

CAP = 2
ROWS = 16
MESH = pl.DeviceIdType.MESH


def kernel(
    tab, inter_s, inter_v, keys, shared, owned, ops, out,
    sh0, sh1, sh2, sh3, ow, opv, send, recv, keyr, kron, dn, dp, y, pbs, pbr, acc, outb, ipv, ips,
    sh_sem, ow_sem, op_sem, send_sem, recv_sem, ksend_sem, krecv_sem,
    isend_sem, irecv_sem, ips_sem, as_sem, ar_sem, bs_sem, br_sem, out_sem,
):
    sh = (sh0, sh1, sh2, sh3)
    chunks, octs, rows, width = dn.shape
    peers = recv.shape[1]
    lps = opv.shape[1]
    slab = lax.axis_index("slab")
    cube = lax.axis_index("cube")
    x, z, core = cube // 8, (cube // 2) % 4, cube % 2
    swap = slab + 1 - 2 * (slab % 2)
    pair_a = core * (3 - slab) + (1 - core) * swap
    pair_b = core * swap + (1 - core) * (3 - slab)

    def offset(step):
        return (step * 13) % peers

    def peer(r):
        return ((x + r // 8) % 4) * 8 + ((z + (r // 2) % 4) % 4) * 2 + (core + r % 2) % 2

    def sh_copy(q):
        return pltpu.make_async_copy(
            shared.at[:, pl.ds(q * rows, rows), :], sh[q], sh_sem.at[q])

    def ow_copy(q):
        return pltpu.make_async_copy(
            owned.at[:, pl.ds(q * rows, rows), :], ow.at[q], ow_sem.at[q])

    def op_copy(i, s):
        return pltpu.make_async_copy(
            ops.at[pl.ds(s * lps, lps)], opv.at[i], op_sem.at[i])

    def out_copy(q):
        return pltpu.make_async_copy(
            outb.at[q], out.at[:, pl.ds(q * rows, rows), :], out_sem.at[q])

    def a_copy(q):
        return pltpu.make_async_remote_copy(
            dn.at[q], dp.at[q], as_sem.at[q], ar_sem.at[q],
            device_id=(pair_a, cube), device_id_type=MESH)

    def b_copy(q):
        return pltpu.make_async_remote_copy(
            pbs.at[q], pbr.at[q], bs_sem.at[q], br_sem.at[q],
            device_id=(pair_b, cube), device_id_type=MESH)

    def i_copy():
        return pltpu.make_async_remote_copy(
            inter_v, ipv, isend_sem, irecv_sem,
            device_id=(pair_b, cube), device_id_type=MESH)

    for q in range(chunks):
        sh_copy(q).start()
    for q in range(chunks):
        ow_copy(q).start()
    op_copy(0, slab).start()
    op_copy(1, pair_a).start()

    barrier = pltpu.get_barrier_semaphore()

    def greet(r, carry):
        pl.semaphore_signal(barrier, inc=1, device_id=(slab, peer(r)), device_id_type=MESH)
        return carry

    lax.fori_loop(1, peers, greet, 0)
    for s in (pair_a, pair_b):
        pl.semaphore_signal(barrier, inc=1, device_id=(s, cube), device_id_type=MESH)

    def pack(q, r, to):
        c = peer(r)
        for k in range(CAP):
            to[q, r, k] = sh[q][tab[c * CAP + k]]

    def pack_step(q, step, carry):
        pack(q, offset(step), send)
        return carry

    def send_step(q, step, carry):
        r = offset(step)
        pltpu.make_async_remote_copy(
            send.at[q, r], recv.at[q, r], send_sem.at[q], recv_sem.at[q],
            device_id=(slab, peer(r)), device_id_type=MESH).start()
        return carry

    def key_step(r, carry):
        c = peer(r)
        pltpu.make_async_remote_copy(
            keys.at[c], keyr.at[r], ksend_sem, krecv_sem,
            device_id=(slab, c), device_id_type=MESH).start()
        return carry

    for q in range(chunks):
        sh_copy(q).wait()
        pack(q, 0, recv)
        lax.fori_loop(1, peers, functools.partial(pack_step, q), 0)
        if q == 0:
            keyr[0] = keys[cube]
            pl.semaphore_wait(barrier, peers + 1)
            lax.fori_loop(1, peers, key_step, 0)
            i_copy().start()
        lax.fori_loop(1, peers, functools.partial(send_step, q), 0)

    far = pl.ds(1, peers - 1)

    def sum_chunk(q):
        pltpu.make_async_copy(recv.at[q, far], recv.at[q, far], recv_sem.at[q]).wait()
        ow_copy(q).wait()
        total = jnp.dot(
            kron[...], recv[q].reshape(peers * CAP * rows, width),
            preferred_element_type=jnp.float32)
        total = total + ow[q].reshape(octs * rows, width).astype(jnp.float32)
        dn[q] = total.astype(jnp.bfloat16).reshape(octs, rows, width)

    def products(i, src, q):
        def one(e, carry):
            prod = jnp.dot(
                src[q].reshape(octs * rows, width), opv[i, e],
                preferred_element_type=jnp.float32)
            y[i, pl.ds(e * octs, octs)] = prod.reshape(octs, rows, width)
            return carry
        lax.fori_loop(0, lps, one, 0)

    def gather(table, t):
        row, base = t // 4, (t % 4) * 32
        total = None
        for i, s in ((0, slab), (1, pair_a)):
            for e in range(lps):
                term = y[i, e * octs + table[row, base + s * lps + e]]
                total = term if total is None else total + term
        return total

    def finish(q):
        b_copy(q).wait_recv()
        outb[q] = (acc[q] + pbr[q].astype(jnp.float32)).astype(jnp.bfloat16)
        out_copy(q).start()

    for q in range(chunks):
        if q == 0:
            pltpu.make_async_copy(keyr.at[far], keyr.at[far], krecv_sem).wait()
            lane = lax.broadcasted_iota(jnp.int32, (1, 128), 1) // 32
            line = lax.broadcasted_iota(jnp.int32, (octs * rows, 128), 0)
            for g in range(peers // 4):
                key = keyr[4 * g]
                for b in range(1, 4):
                    key = jnp.where(lane == b, keyr[4 * g + b], key)
                kron[:, pl.ds(g * 128, 128)] = jnp.where(
                    key == line, 1.0, 0.0).astype(jnp.bfloat16)
        sum_chunk(q)
        a_copy(q).start()
        if q == 0:
            i_copy().wait_recv()
            to_smem = pltpu.make_async_copy(ipv, ips, ips_sem)
            to_smem.start()
            to_smem.wait()
            op_copy(0, slab).wait()
        else:
            finish(q - 1)
        products(0, dn, q)
        if q == 0:
            op_copy(1, pair_a).wait()
        a_copy(q).wait_recv()
        products(1, dp, q)

        def partner_target(t, carry, q=q):
            pbs[q, t] = gather(ips, t).astype(jnp.bfloat16)
            return carry

        lax.fori_loop(0, octs, partner_target, 0)
        b_copy(q).start()

        def own_target(t, carry, q=q):
            acc[q, t] = gather(inter_s, t)
            return carry

        lax.fori_loop(0, octs, own_target, 0)
    finish(chunks - 1)
    for q in range(chunks):
        pltpu.make_async_copy(send.at[q, far], send.at[q, far], send_sem.at[q]).wait()
        a_copy(q).wait_send()
        b_copy(q).wait_send()
        out_copy(q).wait()
    pltpu.make_async_copy(keyr.at[far], keyr.at[far], ksend_sem).wait()
    i_copy().wait_send()


def body(owned_part, shared_part, shared_cube, shared_octant, interaction, operators):
    octs, rhs, width = owned_part.shape
    slots = shared_part.shape[0]
    slabs, lps = interaction.shape[1:]
    cubes = lax.axis_size("cube")
    chunks = rhs // ROWS
    owner = shared_cube[:, 0]
    order = jnp.arange(slots, dtype=jnp.int32)
    earlier = (owner[:, None] == owner[None, :]) & (order[None, :] < order[:, None])
    rank = jnp.sum(earlier.astype(jnp.int32), axis=1)
    position = owner * CAP + rank
    placing = jnp.arange(cubes * CAP, dtype=jnp.int32)[:, None] == position[None, :]
    tab = jnp.sum(jnp.where(placing, order[None, :], 0), axis=1)
    label = jnp.sum(jnp.where(placing, shared_octant[None, :] + 1, 0), axis=1) - 1
    spread = jnp.arange(ROWS, dtype=jnp.int32)[None, None, None, :]
    label = label.reshape(cubes, 1, CAP, 1)
    keys = jnp.where(label >= 0, label * ROWS + spread, -1)
    keys = jnp.broadcast_to(keys, (cubes, 4, CAP, ROWS)).reshape(cubes, 1, 4 * CAP * ROWS)
    inter = interaction.reshape(octs // 4, 4 * slabs * lps)
    bf16, f32, dma = jnp.bfloat16, jnp.float32, pltpu.SemaphoreType.DMA
    block = (chunks, octs, ROWS, width)
    smem = pl.BlockSpec(memory_space=pltpu.SMEM)
    vmem = pl.BlockSpec(memory_space=pltpu.VMEM)
    hbm = pl.BlockSpec(memory_space=pl.ANY)
    return pl.pallas_call(
        kernel,
        out_shape=jax.ShapeDtypeStruct((octs, rhs, width), bf16),
        in_specs=[smem, smem, vmem, vmem, hbm, hbm, hbm],
        out_specs=hbm,
        scratch_shapes=[
            *[pltpu.VMEM((slots, ROWS, width), bf16) for _ in range(chunks)],
            pltpu.VMEM(block, bf16),
            pltpu.VMEM((2, lps, width, width), bf16),
            pltpu.VMEM((chunks, cubes, CAP, ROWS, width), bf16),
            pltpu.VMEM((chunks, cubes, CAP, ROWS, width), bf16),
            pltpu.VMEM((cubes, 1, 128), jnp.int32),
            pltpu.VMEM((octs * ROWS, cubes * CAP * ROWS), bf16),
            pltpu.VMEM(block, bf16),
            pltpu.VMEM(block, bf16),
            pltpu.VMEM((2, lps * octs, ROWS, width), f32),
            pltpu.VMEM(block, bf16),
            pltpu.VMEM(block, bf16),
            pltpu.VMEM(block, f32),
            pltpu.VMEM(block, bf16),
            pltpu.VMEM(inter.shape, jnp.int32),
            pltpu.SMEM(inter.shape, jnp.int32),
            dma((chunks,)), dma((chunks,)), dma((2,)), dma((chunks,)), dma((chunks,)),
            dma, dma, dma, dma, dma,
            dma((chunks,)), dma((chunks,)), dma((chunks,)), dma((chunks,)), dma((chunks,)),
        ],
        compiler_params=pltpu.CompilerParams(
            collective_id=0, has_side_effects=True, vmem_limit_bytes=56 * 2**20),
        cost_estimate=pl.CostEstimate(
            flops=2 * 2 * lps * octs * rhs * width * width,
            bytes_accessed=20 * 2**20, transcendentals=0),
    )(tab, inter, inter, keys, shared_part, owned_part, operators)


def solution(mesh):
    placed = (
        P(("slab", "cube"), None, None),
        P(("slab", "cube"), None, None),
        P(("slab", "cube"), None),
        P(("slab", "cube")),
        P(("slab", "cube"), None, None),
        P(),
    )
    return jax.shard_map(
        body, mesh=mesh, in_specs=placed, out_specs=P(("slab", "cube"), None, None), check_vma=False
    )
```

time: 528 us -> 105 us (0.20); the launches traced: 519 us -> 104 us
  waiting for transfers between devices: 209 us -> 0 us
  matrix products: 129 us -> 0 us
  local copies, waits for them, and re-layouts: 115 us -> 5.3 us
  Pallas kernels: 0 us -> 96.8 us
  other arithmetic: 32.1 us -> 2.28 us
  starting transfers between devices: 19 us -> 0 us
  between operations: 14.4 us -> 0.04 us
    ppermute x10 -> x0, waiting for transfers between devices: 142 us -> none  [swapped(): return lax.ppermute(value, axis, pairs)]
    dot_general x34 -> x0, matrix products: 129 us -> none  [the longest x32 125 us: body(): jnp.dot(selected, operator_now, preferred_element_type=jnp.float32)]
    pallas_call x0 -> x1, Pallas kernels: none -> 96.8 us  [body(): pl.pallas_call(kernel, out_shape=jax.ShapeDtypeStruct((octs, rhs, width),...]
    gather x32 -> x0, local copies, waits for them, and re-layouts: 83.2 us -> none  [body(): jnp.take(shard_rows, sources[:, entry], axis=0)]
    all_gather x1 -> x0, waiting for transfers between devices: 66.3 us -> none  [body(): shard_block = lax.all_gather(density, 'slab', axis=0, tiled=True)]
    concatenate x7 -> x0, other arithmetic: 24.8 us -> none  [the longest x4 24.6 us: body(): buffer = jnp.concatenate([retained, incoming], axis=1)]
    ppermute x10 -> x0, starting transfers between devices: 19 us -> none  [swapped(): return lax.ppermute(value, axis, pairs)]
    unnamed x86 -> x2, local copies, waits for them, and re-layouts: 12.9 us -> 3.51 us
  transfers between devices with their start and end apart: 11 -> 0, of which waited for: 9 -> 0; matrix products, arithmetic and copies ran while one was open for 1% -> 0% of each run, Pallas kernels for 0% -> 0%
where the time goes in v1:
time: 105 us; the launch traced here: 104 us
  Pallas kernels  96.8 us (92%)
  local copies, waits for them, and re-layouts  5.3 us (5%)
  other arithmetic  2.28 us (2%)
    pallas_call x1, Pallas kernels, body(): pl.pallas_call(kernel, out_shape=jax.ShapeDtypeStruct((octs, rhs, width),...  96.8 us
    unnamed x2, local copies, waits for them, and re-layouts  3.51 us

profile of v1, /device:TPU:0, one launch (start us, length us, event | category | flops | bytes accessed | tf_op | source)
XLA Modules:
  0.0 104.5 jit_solution(13708494727159858742)
XLA Ops:
  0.0 0.9 convert_reduce_fusion
  0.9 0.7 multiply_add_fusion
  1.6 0.7 select_reduce_fusion
  2.3 0.1 ge.16
  2.4 0.1 copy.13
  2.5 0.1 mul.28
  2.6 0.1 copy.14
  2.7 0.7 copy.15.keys
  3.4 0.8 copy.12
  4.2 0.7 reshape.51.inter_s.inter_v
  4.9 96.8 %shard_map.64 = bf16[32,64,384]{2,1,0:T(8,128)(2,1)} custom-call(s32[64]{0:T(128)} %get-tuple-element.6.tab, s32[8,128]{1,0:T(8,128)} %reshape.51.inter_s.inter_v, s32[8,128]{1,0:T(8,128)} %reshape.51.inter_s.inter_v, s32[32,1,128]{2,1,0:T(1,128)} %copy.15.keys, bf16[32,64,384]{2,1,0:T(8,128)(2,1)} %shared.1, bf16[32,64,384]{2,1,0:T(8,128)(2,1)} %owned.1, ...), custom_call_target="tpu_custom_call" | custom-call | flops 9663676416 | bytes 20971520 | tf_op jit(solution)/shard_map/pallas_call | solution.py:227
  101.8 2.7 %copy.17 = bf16[32,64,384]{2,1,0:T(8,128)(2,1)} copy(bf16[32,64,384]{2,1,0:T(8,128)(2,1)} %shard_map.64) | data formatting | bytes 3145728
  (4 shorter events, 0.0 us)

commit v2 on v0

v2 whole, which is shorter than its diff:
```python
import jax
import jax.numpy as jnp
from jax import lax
from jax.experimental import pallas as pl
from jax.experimental.pallas import tpu as pltpu
from jax.sharding import PartitionSpec as P

CAP = 2
ROWS = 16
AHEAD = 4
GROUP = 4
MESH = pl.DeviceIdType.MESH


def kernel(inter_s, inter_v, cube_row, octant_row, shared, owned, ops, out, *scratch):
    count = out.shape[1] // ROWS
    blocks = count
    rows = ROWS
    scratch = list(scratch)

    def take(n):
        taken = scratch[:n]
        del scratch[:n]
        return taken

    sh, ow, outb = take(blocks), take(blocks), take(blocks)
    send, recv = take(count), take(count)
    dn, dp, pbs, pbr, acc = take(count), take(count), take(count), take(count), take(count)
    opv, y, kron, tabv, tabs, keyv, keyr, ipv, ips = take(9)
    sh_sem, ow_sem, op_sem, out_sem, send_sem, recv_sem, as_sem, ar_sem, bs_sem, br_sem = take(10)
    ksend_sem, krecv_sem, isend_sem, irecv_sem, ips_sem, tab_sem = take(6)

    octs, _, width = out.shape
    slots = shared.shape[0]
    peers = keyr.shape[0]
    lps = opv.shape[1] * GROUP
    slab = lax.axis_index("slab")
    cube = lax.axis_index("cube")
    x, z, core = lax.div(cube, 8), lax.rem(lax.div(cube, 2), 4), lax.rem(cube, 2)
    swap = slab + 1 - 2 * lax.rem(slab, 2)
    pair_a = core * (3 - slab) + (1 - core) * swap
    pair_b = core * swap + (1 - core) * (3 - slab)

    at_x = [lax.rem(x + d, 4) * 8 for d in range(4)]
    at_z = [lax.rem(z + d, 4) * 2 for d in range(4)]
    at_core = [core, 1 - core]

    def peer(r):
        return at_x[r // 8] + at_z[r // 2 % 4] + at_core[r % 2]

    order = [step * 13 % peers for step in range(1, peers)]

    def sh_copy(b):
        return pltpu.make_async_copy(
            shared.at[:, pl.ds(b * ROWS, ROWS), :], sh[b], sh_sem.at[b])

    def ow_copy(b):
        return pltpu.make_async_copy(
            owned.at[:, pl.ds(b * ROWS, ROWS), :], ow[b], ow_sem.at[b])

    def op_copy(i, s, e):
        h, j = e // GROUP, e % GROUP
        return pltpu.make_async_copy(
            ops.at[s * lps + e], opv.at[i, h, :, pl.ds(j * width, width)], op_sem.at[i, e])

    def out_copy(b):
        return pltpu.make_async_copy(
            outb[b], out.at[:, pl.ds(b * ROWS, ROWS), :], out_sem.at[b])

    def a_copy(u):
        return pltpu.make_async_remote_copy(
            dn[u], dp[u], as_sem.at[u], ar_sem.at[u],
            device_id=(pair_a, cube), device_id_type=MESH)

    def b_copy(u):
        return pltpu.make_async_remote_copy(
            pbs[u], pbr[u], bs_sem.at[u], br_sem.at[u],
            device_id=(pair_b, cube), device_id_type=MESH)

    def i_copy():
        return pltpu.make_async_remote_copy(
            inter_v, ipv, isend_sem, irecv_sem,
            device_id=(pair_b, cube), device_id_type=MESH)

    for b in range(blocks):
        sh_copy(b).start()
    for b in range(blocks):
        ow_copy(b).start()
    for i, s in ((0, slab), (1, pair_a)):
        for e in range(lps):
            op_copy(i, s, e).start()

    barrier = pltpu.get_barrier_semaphore()

    for r in order:
        pl.semaphore_signal(barrier, inc=1, device_id=(slab, peer(r)), device_id_type=MESH)
    for s in (pair_a, pair_b):
        pl.semaphore_signal(barrier, inc=1, device_id=(s, cube), device_id_type=MESH)

    line = lax.broadcasted_iota(jnp.int32, (slots, slots), 0)
    lane = lax.broadcasted_iota(jnp.int32, (slots, slots), 1)

    def column(row):
        spread = jnp.broadcast_to(row, (slots, slots))
        return jnp.sum(jnp.where(line == lane, spread, 0), axis=1, keepdims=True)

    owner = cube_row[...]
    owner_col = column(owner)
    octant_col = column(octant_row[...])
    rank_col = jnp.sum(
        jnp.where((owner_col == owner) & (lane < line), 1, 0), axis=1, keepdims=True)
    for k in range(CAP):
        named = (owner_col == lane) & (rank_col == k)
        tabv[k:k + 1, 0:slots] = jnp.sum(jnp.where(named, line, 0), axis=0, keepdims=True)
    to_tabs = pltpu.make_async_copy(tabv, tabs, tab_sem)
    to_tabs.start()
    goes = jnp.where(owner == line, 1.0, 0.0).astype(jnp.bfloat16)
    wide = lax.broadcasted_iota(jnp.int32, (slots, 128), 1)
    value = jnp.where(rank_col == (wide // rows) % CAP, octant_col + 1, 0)
    label = jnp.dot(
        goes, value.astype(jnp.bfloat16),
        preferred_element_type=jnp.float32).astype(jnp.int32) - 1
    key = jnp.where(label >= 0, label * rows + wide % rows, -1)
    for c in range(peers):
        keyv[c] = key[c:c + 1, :]
    to_tabs.wait()

    def pack_unit(u):
        sh_copy(u).wait()
        for r in [0] + order:
            c = peer(r)
            to = send if r else recv
            for k in range(CAP):
                to[u][r, k * rows:(k + 1) * rows] = sh[u][tabs[k, c]]

    def send_unit(u):
        for r in order:
            pltpu.make_async_remote_copy(
                send[u].at[r], recv[u].at[r], send_sem.at[u], recv_sem.at[u],
                device_id=(slab, peer(r)), device_id_type=MESH).start()

    pack_unit(0)
    keyr[0] = keyv[cube]
    pl.semaphore_wait(barrier, peers + 1)
    for r in order:
        pltpu.make_async_remote_copy(
            keyv.at[peer(r)], keyr.at[r], ksend_sem, krecv_sem,
            device_id=(slab, peer(r)), device_id_type=MESH).start()
    i_copy().start()
    send_unit(0)
    for u in range(1, AHEAD):
        pack_unit(u)
        send_unit(u)

    far = pl.ds(1, peers - 1)

    def build():
        span = CAP * rows
        each = 128 // span
        spot = lax.broadcasted_iota(jnp.int32, (1, 128), 1) // span
        row = lax.broadcasted_iota(jnp.int32, (octs * rows, 128), 0)
        for g in range(peers // each):
            key = keyr[each * g]
            for i in range(1, each):
                key = jnp.where(spot == i, keyr[each * g + i], key)
            kron[:, pl.ds(g * 128, 128)] = jnp.where(key == row, 1.0, 0.0).astype(jnp.bfloat16)

    def sum_unit(u):
        pltpu.make_async_copy(recv[u].at[far], recv[u].at[far], recv_sem.at[u]).wait()
        ow_copy(u).wait()
        total = jnp.dot(
            kron[...], recv[u][...].reshape(peers * CAP * rows, width),
            preferred_element_type=jnp.float32)
        total = total + ow[u][...].reshape(octs * rows, width).astype(jnp.float32)
        dn[u][...] = total.astype(jnp.bfloat16)

    def products(i, u):
        src = (dn, dp)[i][u]

        def one(h, carry):
            prod = jnp.dot(src[...], opv[i, h], preferred_element_type=jnp.float32)
            for j in range(GROUP):
                y[i, pl.ds((h * GROUP + j) * octs, octs)] = prod[
                    :, j * width:(j + 1) * width].reshape(octs, rows, width)
            return carry

        lax.fori_loop(0, lps // GROUP, one, 0)

    def gather(table, t):
        total = None
        for i, s in ((0, slab), (1, pair_a)):
            for e in range(lps):
                term = y[i, e * octs + table[s * lps + e, t]]
                total = term if total is None else total + term
        return total

    def gather_partner(u):
        def step(t, carry):
            pbs[u][t] = gather(ips, t).astype(jnp.bfloat16)
            return carry

        lax.fori_loop(0, octs, step, 0)

    def gather_own(u):
        def step(t, carry):
            acc[u][t] = gather(inter_s, t)
            return carry

        lax.fori_loop(0, octs, step, 0)

    def finish(u):
        b_copy(u).wait_recv()
        outb[u][...] = (acc[u][...] + pbr[u][...].astype(jnp.float32)).astype(jnp.bfloat16)
        out_copy(u).start()

    def second(u):
        a_copy(u).wait_recv()
        products(1, u)
        gather_partner(u)
        b_copy(u).start()

    pltpu.make_async_copy(keyr.at[far], keyr.at[far], krecv_sem).wait()
    build()
    for u in range(count):
        sum_unit(u)
        a_copy(u).start()
        if u + AHEAD < count:
            pack_unit(u + AHEAD)
            send_unit(u + AHEAD)
        if u == 0:
            i_copy().wait_recv()
            to_smem = pltpu.make_async_copy(ipv, ips, ips_sem)
            to_smem.start()
            to_smem.wait()
            for i, s in ((0, slab), (1, pair_a)):
                for e in range(lps):
                    op_copy(i, s, e).wait()
        if 0 < u < count - 1:
            second(u - 1)
        if u > 0:
            gather_own(u - 1)
        if u > 1:
            finish(u - 2)
        products(0, u)
        if u >= count - 2:
            second(u)
    gather_own(count - 1)
    finish(count - 2)
    finish(count - 1)
    for u in range(count):
        pltpu.make_async_copy(send[u].at[far], send[u].at[far], send_sem.at[u]).wait()
        a_copy(u).wait_send()
        b_copy(u).wait_send()
    for b in range(blocks):
        out_copy(b).wait()
    pltpu.make_async_copy(keyv.at[far], keyv.at[far], ksend_sem).wait()
    i_copy().wait_send()


def body(owned_part, shared_part, shared_cube, shared_octant, interaction, operators):
    octs, rhs, width = owned_part.shape
    slots = shared_part.shape[0]
    slabs, lps = interaction.shape[1:]
    cubes = lax.axis_size("cube")
    blocks = count = rhs // ROWS
    inter = interaction.transpose(1, 2, 0).reshape(slabs * lps, octs)
    bf16, f32, i32, dma = jnp.bfloat16, jnp.float32, jnp.int32, pltpu.SemaphoreType.DMA
    smem = pl.BlockSpec(memory_space=pltpu.SMEM)
    vmem = pl.BlockSpec(memory_space=pltpu.VMEM)
    hbm = pl.BlockSpec(memory_space=pl.ANY)
    routed = [pltpu.VMEM((cubes, CAP * ROWS, width), bf16)] * count
    flat = [pltpu.VMEM((octs * ROWS, width), bf16)] * count
    partial = [pltpu.VMEM((octs, ROWS, width), bf16)] * count
    total = [pltpu.VMEM((octs, ROWS, width), f32)] * count
    return pl.pallas_call(
        kernel,
        out_shape=jax.ShapeDtypeStruct((octs, rhs, width), bf16),
        in_specs=[smem, vmem, vmem, vmem, hbm, hbm, hbm],
        out_specs=hbm,
        scratch_shapes=[
            *[pltpu.VMEM((slots, ROWS, width), bf16) for _ in range(blocks)],
            *[pltpu.VMEM((octs, ROWS, width), bf16) for _ in range(2 * blocks)],
            *routed, *routed, *flat, *flat, *partial, *partial, *total,
            pltpu.VMEM((2, lps // GROUP, width, GROUP * width), bf16),
            pltpu.VMEM((2, lps * octs, ROWS, width), f32),
            pltpu.VMEM((octs * ROWS, cubes * CAP * ROWS), bf16),
            pltpu.VMEM((8, 128), i32),
            pltpu.SMEM((8, 128), i32),
            pltpu.VMEM((cubes, 1, 128), i32),
            pltpu.VMEM((cubes, 1, 128), i32),
            pltpu.VMEM(inter.shape, i32),
            pltpu.SMEM(inter.shape, i32),
            dma((blocks,)), dma((blocks,)), dma((2, lps)), dma((blocks,)),
            *[dma((count,)) for _ in range(6)],
            *[dma for _ in range(6)],
        ],
        compiler_params=pltpu.CompilerParams(
            collective_id=0, has_side_effects=True, vmem_limit_bytes=56 * 2**20),
        cost_estimate=pl.CostEstimate(
            flops=2 * 2 * lps * octs * rhs * width * width,
            bytes_accessed=20 * 2**20, transcendentals=0),
    )(inter, inter, shared_cube.reshape(1, slots), shared_octant.reshape(1, slots),
      shared_part, owned_part, operators)


def solution(mesh):
    placed = (
        P(("slab", "cube"), None, None),
        P(("slab", "cube"), None, None),
        P(("slab", "cube"), None),
        P(("slab", "cube")),
        P(("slab", "cube"), None, None),
        P(),
    )
    return jax.shard_map(
        body, mesh=mesh, in_specs=placed, out_specs=P(("slab", "cube"), None, None), check_vma=False
    )
```

time: 528 us -> 74.1 us (0.14); the launches traced: 519 us -> 73.9 us
  waiting for transfers between devices: 209 us -> 0 us
  matrix products: 129 us -> 0 us
  local copies, waits for them, and re-layouts: 115 us -> 2.71 us
  Pallas kernels: 0 us -> 71.2 us
  other arithmetic: 32.1 us -> 0 us
  starting transfers between devices: 19 us -> 0 us
  between operations: 14.4 us -> 0.01 us
    ppermute x10 -> x0, waiting for transfers between devices: 142 us -> none  [swapped(): return lax.ppermute(value, axis, pairs)]
    dot_general x34 -> x0, matrix products: 129 us -> none  [the longest x32 125 us: body(): jnp.dot(selected, operator_now, preferred_element_type=jnp.float32)]
    gather x32 -> x0, local copies, waits for them, and re-layouts: 83.2 us -> none  [body(): jnp.take(shard_rows, sources[:, entry], axis=0)]
    pallas_call x0 -> x1, Pallas kernels: none -> 71.2 us  [body(): pl.pallas_call(kernel, out_shape=jax.ShapeDtypeStruct((octs, rhs, width),...]
    all_gather x1 -> x0, waiting for transfers between devices: 66.3 us -> none  [body(): shard_block = lax.all_gather(density, 'slab', axis=0, tiled=True)]
    concatenate x7 -> x0, other arithmetic: 24.8 us -> none  [the longest x4 24.6 us: body(): buffer = jnp.concatenate([retained, incoming], axis=1)]
    ppermute x10 -> x0, starting transfers between devices: 19 us -> none  [swapped(): return lax.ppermute(value, axis, pairs)]
    unnamed x86 -> x1, local copies, waits for them, and re-layouts: 12.9 us -> 2.71 us
  transfers between devices with their start and end apart: 11 -> 0, of which waited for: 9 -> 0; matrix products, arithmetic and copies ran while one was open for 1% -> 0% of each run, Pallas kernels for 0% -> 0%
where the time goes in v2:
time: 74.1 us; the launch traced here: 73.9 us
  Pallas kernels  71.2 us (96%)
  local copies, waits for them, and re-layouts  2.71 us (4%)
    pallas_call x1, Pallas kernels, body(): pl.pallas_call(kernel, out_shape=jax.ShapeDtypeStruct((octs, rhs, width),...  71.2 us
    unnamed x1, local copies, waits for them, and re-layouts  2.71 us

profile of v2, /device:TPU:0, one launch (start us, length us, event | category | flops | bytes accessed | tf_op | source)
XLA Modules:
  0.0 73.9 jit_solution(6269056893732155036)
XLA Ops:
  0.0 71.2 %shard_map.64 = bf16[32,64,384]{2,1,0:T(8,128)(2,1)} custom-call(s32[32,32]{1,0:T(8,128)} %bitcast.5, s32[32,32]{1,0:T(8,128)} %bitcast.6, s32[1,32]{1,0:T(1,128)} %bitcast.7, s32[1,32]{1,0:T(1,128)} %bitcast.8, bf16[32,64,384]{2,1,0:T(8,128)(2,1)} %shared.1, bf16[32,64,384]{2,1,0:T(8,128)(2,1)} %owned.1, bf16[32,384,384]{2,1,0:T(8,128)(2,1)} %ops.1), custom_call_target="tpu_custom_call" | custom-call | flops 9663676416 | bytes 20971520 | tf_op jit(solution)/shard_map/pallas_call | solution.py:275
  71.2 2.7 %copy.8 = bf16[32,64,384]{2,1,0:T(8,128)(2,1)} copy(bf16[32,64,384]{2,1,0:T(8,128)(2,1)} %shard_map.64) | data formatting | bytes 3145728

commit v3 on v2

v3 whole, which is shorter than its diff:
```python
import jax
import jax.numpy as jnp
from jax import lax
from jax.experimental import pallas as pl
from jax.experimental.pallas import tpu as pltpu
from jax.sharding import PartitionSpec as P

CAP = 2
ROWS = 16
UNITS = ((0, 0, 16), (1, 0, 16), (2, 0, 16), (3, 0, 8), (3, 8, 8))
GROUP = 4
MESH = pl.DeviceIdType.MESH


def kernel(inter, cube_row, octant_row, shared, owned, ops, out, *scratch):
    count = len(UNITS)
    blocks = out.shape[1] // ROWS
    scratch = list(scratch)

    def take(n):
        taken = scratch[:n]
        del scratch[:n]
        return taken

    sh, ow = take(blocks), take(blocks)
    send, recv = take(count), take(count)
    dn, dp, pbs, pbr, acc = take(count), take(count), take(count), take(count), take(count)
    opv, y, kron16, kron8, tabv, tabs, keyv, keyr, ipv, ips, inter_s = take(11)
    sh_sem, ow_sem, op_sem, send_sem, recv_sem, as_sem, ar_sem, bs_sem, br_sem = take(9)
    ksend_sem, krecv_sem, isend_sem, irecv_sem, ips_sem, tab_sem, ins_sem = take(7)

    octs, _, width = out.shape
    slots = shared.shape[0]
    peers = keyr.shape[0]
    lps = opv.shape[1] * GROUP
    slab = lax.axis_index("slab")
    cube = lax.axis_index("cube")
    x, z, core = lax.div(cube, 8), lax.rem(lax.div(cube, 2), 4), lax.rem(cube, 2)
    swap = slab + 1 - 2 * lax.rem(slab, 2)
    pair_a = core * (3 - slab) + (1 - core) * swap
    pair_b = core * swap + (1 - core) * (3 - slab)

    at_x = [lax.rem(x + d, 4) * 8 for d in range(4)]
    at_z = [lax.rem(z + d, 4) * 2 for d in range(4)]
    at_core = [core, 1 - core]

    def peer(r):
        return at_x[r // 8] + at_z[r // 2 % 4] + at_core[r % 2]

    order = [step * 13 % peers for step in range(1, peers)]

    def sh_copy(b):
        return pltpu.make_async_copy(
            shared.at[:, pl.ds(b * ROWS, ROWS), :], sh[b], sh_sem.at[b])

    def ow_copy(b):
        return pltpu.make_async_copy(
            owned.at[:, pl.ds(b * ROWS, ROWS), :], ow[b], ow_sem.at[b])

    def op_copy(i, s, e):
        h, j = e // GROUP, e % GROUP
        return pltpu.make_async_copy(
            ops.at[s * lps + e], opv.at[i, h, :, pl.ds(j * width, width)], op_sem.at[i, e])

    def a_copy(u):
        return pltpu.make_async_remote_copy(
            dn[u], dp[u], as_sem.at[u], ar_sem.at[u],
            device_id=(pair_a, cube), device_id_type=MESH)

    def b_copy(u):
        return pltpu.make_async_remote_copy(
            pbs[u], pbr[u], bs_sem.at[u], br_sem.at[u],
            device_id=(pair_b, cube), device_id_type=MESH)

    def i_copy():
        return pltpu.make_async_remote_copy(
            inter, ipv, isend_sem, irecv_sem,
            device_id=(pair_b, cube), device_id_type=MESH)

    sh_copy(0).start()
    barrier = pltpu.get_barrier_semaphore()

    for r in order:
        pl.semaphore_signal(barrier, inc=1, device_id=(slab, peer(r)), device_id_type=MESH)
    for s in (pair_a, pair_b):
        pl.semaphore_signal(barrier, inc=1, device_id=(s, cube), device_id_type=MESH)
    for b in range(1, blocks):
        sh_copy(b).start()

    line = lax.broadcasted_iota(jnp.int32, (slots, slots), 0)
    lane = lax.broadcasted_iota(jnp.int32, (slots, slots), 1)

    def column(row):
        spread = jnp.broadcast_to(row, (slots, slots))
        return jnp.sum(jnp.where(line == lane, spread, 0), axis=1, keepdims=True)

    owner = cube_row[...]
    owner_col = column(owner)
    octant_col = column(octant_row[...])
    rank_col = jnp.sum(
        jnp.where((owner_col == owner) & (lane < line), 1, 0), axis=1, keepdims=True)
    for k in range(CAP):
        named = (owner_col == lane) & (rank_col == k)
        tabv[k:k + 1, 0:slots] = jnp.sum(jnp.where(named, line, 0), axis=0, keepdims=True)
    to_tabs = pltpu.make_async_copy(tabv, tabs, tab_sem)
    to_tabs.start()
    to_tabs.wait()

    def pack_unit(u):
        b, first, rows = UNITS[u]
        if first == 0:
            sh_copy(b).wait()
        for r in [0] + order:
            c = peer(r)
            to = send if r else recv
            if rows == ROWS:
                for k in range(CAP):
                    to[u][r, k * rows:(k + 1) * rows] = sh[b][tabs[k, c]]
            else:
                parts = [
                    sh[b][tabs[k, c]].astype(jnp.float32)[first:first + rows]
                    for k in range(CAP)]
                to[u][r] = jnp.concatenate(parts, axis=0).astype(jnp.bfloat16)

    def send_unit(u):
        for r in order:
            pltpu.make_async_remote_copy(
                send[u].at[r], recv[u].at[r], send_sem.at[u], recv_sem.at[u],
                device_id=(slab, peer(r)), device_id_type=MESH).start()

    pack_unit(0)
    pl.semaphore_wait(barrier, peers + 1)
    send_unit(0)
    goes = jnp.where(owner == line, 1.0, 0.0).astype(jnp.bfloat16)
    wide = lax.broadcasted_iota(jnp.int32, (slots, 128), 1)
    for i, rows in enumerate((16, 8)):
        value = jnp.where(rank_col == (wide // rows) % CAP, octant_col + 1, 0)
        label = jnp.dot(
            goes, value.astype(jnp.bfloat16),
            preferred_element_type=jnp.float32).astype(jnp.int32) - 1
        key = jnp.where(label >= 0, label * rows + wide % rows, -1)
        for c in range(peers):
            keyv[c, i:i + 1, :] = key[c:c + 1, :]
    keyr[0] = keyv[cube]
    for r in order:
        pltpu.make_async_remote_copy(
            keyv.at[peer(r)], keyr.at[r], ksend_sem, krecv_sem,
            device_id=(slab, peer(r)), device_id_type=MESH).start()
    i_copy().start()
    to_inter = pltpu.make_async_copy(inter, inter_s, ins_sem)
    to_inter.start()
    for b in range(blocks):
        ow_copy(b).start()
    for i, s in ((0, slab), (1, pair_a)):
        for e in range(lps):
            op_copy(i, s, e).start()
    for u in range(1, count):
        pack_unit(u)
        send_unit(u)

    far = pl.ds(1, peers - 1)

    def build(kron, index, rows):
        span = CAP * rows
        each = 128 // span
        spot = lax.broadcasted_iota(jnp.int32, (1, 128), 1) // span
        row = lax.broadcasted_iota(jnp.int32, (octs * rows, 128), 0)
        for g in range(peers // each):
            key = keyr[each * g, index:index + 1, :]
            for i in range(1, each):
                key = jnp.where(spot == i, keyr[each * g + i, index:index + 1, :], key)
            kron[:, pl.ds(g * 128, 128)] = jnp.where(key == row, 1.0, 0.0).astype(jnp.bfloat16)

    def sum_unit(u):
        b, first, rows = UNITS[u]
        pltpu.make_async_copy(recv[u].at[far], recv[u].at[far], recv_sem.at[u]).wait()
        if first == 0:
            ow_copy(b).wait()
        kron = kron16 if rows == ROWS else kron8
        total = jnp.dot(
            kron[...], recv[u][...].reshape(peers * CAP * rows, width),
            preferred_element_type=jnp.float32)
        own = ow[b][...]
        if rows < ROWS:
            own = own.astype(jnp.float32)[:, first:first + rows]
        total = total + own.reshape(octs * rows, width).astype(jnp.float32)
        dn[u][...] = total.astype(jnp.bfloat16)

    def products(i, u):
        rows = UNITS[u][2]
        src = (dn, dp)[i][u]

        def one(h, carry):
            prod = jnp.dot(src[...], opv[i, h], preferred_element_type=jnp.float32)
            for j in range(GROUP):
                y[i, pl.ds((h * GROUP + j) * octs, octs), 0:rows] = prod[
                    :, j * width:(j + 1) * width].reshape(octs, rows, width)
            return carry

        lax.fori_loop(0, lps // GROUP, one, 0)

    def gather(table, t, rows):
        total = None
        for i, s in ((0, slab), (1, pair_a)):
            for e in range(lps):
                term = y[i, e * octs + table[s * lps + e, t], 0:rows]
                total = term if total is None else total + term
        return total

    def gather_partner(u):
        rows = UNITS[u][2]
        per = ROWS // rows

        def step(t, carry):
            parts = [gather(ips, per * t + i, rows) for i in range(per)]
            part = parts[0] if per == 1 else jnp.concatenate(parts, axis=0)
            pbs[u][t] = part.astype(jnp.bfloat16)
            return carry

        lax.fori_loop(0, octs // per, step, 0)

    def gather_own(u):
        rows = UNITS[u][2]
        per = ROWS // rows

        def step(t, carry):
            for i in range(per):
                acc[u][per * t + i] = gather(inter_s, per * t + i, rows)
            return carry

        lax.fori_loop(0, octs // per, step, 0)

    def finish(u):
        b, first, rows = UNITS[u]
        b_copy(u).wait_recv()
        total = acc[u][...] + pbr[u][...].astype(jnp.float32).reshape(octs, rows, width)
        if rows < ROWS and first == 0:
            acc[u][...] = total
            return
        if rows < ROWS:
            total = jnp.concatenate([acc[u - 1][...], total], axis=1)
        out[:, b * ROWS:(b + 1) * ROWS, :] = total.astype(jnp.bfloat16)

    def second(u):
        a_copy(u).wait_recv()
        products(1, u)
        gather_partner(u)
        b_copy(u).start()

    pltpu.make_async_copy(keyr.at[far], keyr.at[far], krecv_sem).wait()
    build(kron16, 0, 16)
    for u in range(count):
        sum_unit(u)
        a_copy(u).start()
        if u == 0:
            build(kron8, 1, 8)
            to_inter.wait()
            i_copy().wait_recv()
            to_smem = pltpu.make_async_copy(ipv, ips, ips_sem)
            to_smem.start()
            to_smem.wait()
            for i, s in ((0, slab), (1, pair_a)):
                for e in range(lps):
                    op_copy(i, s, e).wait()
        else:
            second(u - 1)
            gather_own(u - 1)
        products(0, u)
        if 1 < u < count - 1:
            finish(u - 2)
    second(count - 1)
    gather_own(count - 1)
    for u in range(count - 3, count):
        finish(u)
    for u in range(count):
        pltpu.make_async_copy(send[u].at[far], send[u].at[far], send_sem.at[u]).wait()
        a_copy(u).wait_send()
        b_copy(u).wait_send()
    pltpu.make_async_copy(keyv.at[far], keyv.at[far], ksend_sem).wait()
    i_copy().wait_send()


def body(owned_part, shared_part, shared_cube, shared_octant, interaction, operators):
    octs, rhs, width = owned_part.shape
    slots = shared_part.shape[0]
    slabs, lps = interaction.shape[1:]
    cubes = lax.axis_size("cube")
    blocks = rhs // ROWS
    count = len(UNITS)
    inter = interaction.transpose(1, 2, 0).reshape(slabs * lps, octs)
    bf16, f32, i32, dma = jnp.bfloat16, jnp.float32, jnp.int32, pltpu.SemaphoreType.DMA
    vmem = pl.BlockSpec(memory_space=pltpu.VMEM)
    hbm = pl.BlockSpec(memory_space=pl.ANY)
    routed = [pltpu.VMEM((cubes, CAP * rows, width), bf16) for _, _, rows in UNITS]
    flat = [pltpu.VMEM((octs * rows, width), bf16) for _, _, rows in UNITS]
    partial = [pltpu.VMEM((octs * rows // ROWS, ROWS, width), bf16) for _, _, rows in UNITS]
    total = [pltpu.VMEM((octs, rows, width), f32) for _, _, rows in UNITS]
    return pl.pallas_call(
        kernel,
        out_shape=pltpu.VMEM((octs, rhs, width), bf16),
        in_specs=[hbm, vmem, vmem, hbm, hbm, hbm],
        out_specs=vmem,
        scratch_shapes=[
            *[pltpu.VMEM((slots, ROWS, width), bf16) for _ in range(blocks)],
            *[pltpu.VMEM((octs, ROWS, width), bf16) for _ in range(blocks)],
            *routed, *routed, *flat, *flat, *partial, *partial, *total,
            pltpu.VMEM((2, lps // GROUP, width, GROUP * width), bf16),
            pltpu.VMEM((2, lps * octs, ROWS, width), f32),
            pltpu.VMEM((octs * 16, cubes * CAP * 16), bf16),
            pltpu.VMEM((octs * 8, cubes * CAP * 8), bf16),
            pltpu.VMEM((8, 128), i32),
            pltpu.SMEM((8, 128), i32),
            pltpu.VMEM((cubes, 2, 128), i32),
            pltpu.VMEM((cubes, 2, 128), i32),
            pltpu.VMEM(inter.shape, i32),
            pltpu.SMEM(inter.shape, i32),
            pltpu.SMEM(inter.shape, i32),
            dma((blocks,)), dma((blocks,)), dma((2, lps)),
            *[dma((count,)) for _ in range(6)],
            *[dma for _ in range(7)],
        ],
        compiler_params=pltpu.CompilerParams(
            collective_id=0, has_side_effects=True, vmem_limit_bytes=56 * 2**20),
        cost_estimate=pl.CostEstimate(
            flops=2 * 2 * lps * octs * rhs * width * width,
            bytes_accessed=20 * 2**20, transcendentals=0),
    )(inter, shared_cube.reshape(1, slots), shared_octant.reshape(1, slots),
      shared_part, owned_part, operators)


def solution(mesh):
    placed = (
        P(("slab", "cube"), None, None),
        P(("slab", "cube"), None, None),
        P(("slab", "cube"), None),
        P(("slab", "cube")),
        P(("slab", "cube"), None, None),
        P(),
    )
    return jax.shard_map(
        body, mesh=mesh, in_specs=placed, out_specs=P(("slab", "cube"), None, None), check_vma=False
    )
```

time: 74.1 us -> 70 us (0.945)
  Pallas kernels: 71.2 us -> 68.7 us
  local copies, waits for them, and re-layouts: 2.71 us -> 1.15 us
    pallas_call x1, Pallas kernels: 71.2 us -> 68.7 us  [body(): pl.pallas_call(kernel, out_shape=pltpu.VMEM((octs, rhs, width), bf16), in...]
    unnamed x1, local copies, waits for them, and re-layouts: 2.71 us -> 1.15 us
where the time goes in v3:
time: 70 us; the launch traced here: 69.8 us
  Pallas kernels  68.7 us (98%)
  local copies, waits for them, and re-layouts  1.15 us (2%)
    pallas_call x1, Pallas kernels, body(): pl.pallas_call(kernel, out_shape=pltpu.VMEM((octs, rhs, width), bf16), in...  68.7 us

profile of v3, /device:TPU:0, one launch (start us, length us, event | category | flops | bytes accessed | tf_op | source)
XLA Modules:
  0.0 69.8 jit_solution(13430417274776761569)
XLA Ops:
  0.0 68.7 %shard_map.64 = bf16[32,64,384]{2,1,0:T(8,128)(2,1)S(1)} custom-call(s32[32,32]{1,0:T(8,128)} %bitcast.5, s32[1,32]{1,0:T(1,128)} %bitcast.6, s32[1,32]{1,0:T(1,128)} %bitcast.7, bf16[32,64,384]{2,1,0:T(8,128)(2,1)} %shared.1, bf16[32,64,384]{2,1,0:T(8,128)(2,1)} %owned.1, bf16[32,384,384]{2,1,0:T(8,128)(2,1)} %ops.1), custom_call_target="tpu_custom_call" | custom-call | flops 9663676416 | bytes 20971520 | tf_op jit(solution)/shard_map/pallas_call | solution.py:298
  68.7 1.1 %copy.8 = bf16[32,64,384]{2,1,0:T(8,128)(2,1)} copy(bf16[32,64,384]{2,1,0:T(8,128)(2,1)S(1)} %shard_map.64) | data formatting | bytes 3145728

commit v4 on v3

--- a/solution.py
+++ b/solution.py
@@ -211,17 +211,18 @@
         rows = UNITS[u][2]
         per = ROWS // rows
 
-        def step(t, carry):
-            parts = [gather(ips, per * t + i, rows) for i in range(per)]
-            part = parts[0] if per == 1 else jnp.concatenate(parts, axis=0)
-            pbs[u][t] = part.astype(jnp.bfloat16)
+        def step(i, carry):
+            for t in (2 * i, 2 * i + 1):
+                parts = [gather(ips, per * t + n, rows) for n in range(per)]
+                part = parts[0] if per == 1 else jnp.concatenate(parts, axis=0)
+                pbs[u][t] = part.astype(jnp.bfloat16)
             return carry
 
-        lax.fori_loop(0, octs // per, step, 0)
+        lax.fori_loop(0, octs // per // 2, step, 0)
 
     def gather_own(u):
         rows = UNITS[u][2]
-        per = ROWS // rows
+        per = 2 * ROWS // rows
 
         def step(t, carry):
             for i in range(per):

time: 70 us -> 69.9 us (level)
  no operation moved by 1% of the time
where the time goes in v4:
time: 69.9 us; the launch traced here: 69.8 us
  Pallas kernels  68.6 us (98%)
  local copies, waits for them, and re-layouts  1.15 us (2%)
    pallas_call x1, Pallas kernels, body(): pl.pallas_call(kernel, out_shape=pltpu.VMEM((octs, rhs, width), bf16), in...  68.6 us

profile of v4, /device:TPU:0, one launch (start us, length us, event | category | flops | bytes accessed | tf_op | source)
XLA Modules:
  0.0 69.8 jit_solution(3235458373599175966)
XLA Ops:
  0.0 68.6 %shard_map.64 = bf16[32,64,384]{2,1,0:T(8,128)(2,1)S(1)} custom-call(s32[32,32]{1,0:T(8,128)} %bitcast.5, s32[1,32]{1,0:T(1,128)} %bitcast.6, s32[1,32]{1,0:T(1,128)} %bitcast.7, bf16[32,64,384]{2,1,0:T(8,128)(2,1)} %shared.1, bf16[32,64,384]{2,1,0:T(8,128)(2,1)} %owned.1, bf16[32,384,384]{2,1,0:T(8,128)(2,1)} %ops.1), custom_call_target="tpu_custom_call" | custom-call | flops 9663676416 | bytes 20971520 | tf_op jit(solution)/shard_map/pallas_call | solution.py:299
  68.6 1.1 %copy.8 = bf16[32,64,384]{2,1,0:T(8,128)(2,1)} copy(bf16[32,64,384]{2,1,0:T(8,128)(2,1)S(1)} %shard_map.64) | data formatting | bytes 3145728
